TPU v7x, 256 devices: a whole 4x4x8 slice. The times are simulated.
256 devices in a mesh: band: 64 (over z, x_lo, y), pc: 4 (over x_hi, core).
Axes of the slice: x: 4 (x_hi: 2, x_lo: 2; x = x_hi * 2 + x_lo), y: 4, z: 8, core: 2. Of those that a mesh axis runs over, the one named last changes fastest.
Arguments:
- planes: bfloat16 [3, 256, 256, 256], P(None, 'band', 'pc'), may hold values from -15 to 15
- cotangent: bfloat16 [3, 256, 256, 256], P(None, 'band', 'pc'), may hold values from -6 to 6
- conv_weight: bfloat16 [9, 256, 256], P(None, 'pc'), may hold values from -0.125 to 0.125
- context_gain: bfloat16 [256], P('pc'), may hold values from 0.5 to 1.5
- step_index: int32 [1], replicated, may hold values from 0 to 999
Outputs:
- block_out: bfloat16 [3, 256, 256, 256], P(None, 'band', 'pc')
- input_grad: bfloat16 [3, 256, 256, 256], P(None, 'band', 'pc')
- weight_grad: float32 [9, 256, 256], P(None, 'pc', 'band')
All inputs are finite; a program needn't handle non-finite values.
Results may differ from a plain program's by a relative error of at most 0.0027.
The roundings to bfloat16 on the way count: a program that leaves them out, or rounds other values in their place, can miss the bound.
Values may be sent and summed in bfloat16 or wider, within the bound.
A program may use at most 64 MiB of HBM per device.

v0:
```python
import math
import jax
import jax.numpy as jnp
from jax import lax
from jax.sharding import PartitionSpec as P

C = 256


def with_halo(block, sides, width):
    for axis, dim in sides:
        count = lax.axis_size(axis)
        forward = [(i, i + 1) for i in range(count - 1)]
        backward = [(target, source) for source, target in forward]
        low = lax.ppermute(
            lax.slice_in_dim(block, block.shape[dim] - width, None, axis=dim), axis, forward
        )
        high = lax.ppermute(lax.slice_in_dim(block, 0, width, axis=dim), axis, backward)
        block = jnp.concatenate([low, block, high], axis=dim)
    return block


def time_embed(step_index, channel_ids, channels):
    moment = step_index[0].astype(jnp.float32)
    frequency = jnp.exp(
        -math.log(10000.0) * (2 * (channel_ids // 2)).astype(jnp.float32) / channels
    )
    phase = moment * frequency
    return jnp.where(channel_ids % 2 == 0, jnp.sin(phase), jnp.cos(phase))


def pooled(values):
    col_sums = jnp.sum(values, axis=1)
    row_sums = jnp.sum(values, axis=3)
    totals = lax.psum(col_sums, "band")
    row_sums_all = lax.all_gather(row_sums[2], "band", axis=0, tiled=True)
    return (totals, row_sums, row_sums_all)


def context(values, first_row, side_cells):
    totals, row_sums, row_sums_all = pooled(values)
    row_count = values.shape[1]
    own_columns = lax.dynamic_slice_in_dim(totals[0], first_row, row_count, 1)
    plane_one = row_sums[1][:, :, None] + jnp.transpose(row_sums_all)[None]
    plane_two = row_sums[0][:, :, None] + totals[2][None]
    plane_three = jnp.transpose(own_columns)[:, :, None] + totals[1][None]
    return jnp.stack([plane_one, plane_two, plane_three]) / side_cells


def convolve(values, weight, row_count, col_count):
    total = jnp.zeros((3, row_count, weight.shape[1], col_count), jnp.float32)
    for row_tap in range(3):
        for col_tap in range(3):
            window = values[:, row_tap : row_tap + row_count, :, col_tap : col_tap + col_count]
            total = total + jnp.einsum(
                "oc,kicj->kioj",
                weight[3 * row_tap + col_tap],
                window,
                preferred_element_type=jnp.float32,
            )
    return total


def transposed(values, weight, row_count, col_count):
    total = jnp.zeros((3, row_count, weight.shape[2], col_count), jnp.float32)
    for row_tap in range(3):
        for col_tap in range(3):
            window = values[
                :, 2 - row_tap : 2 - row_tap + row_count, :, 2 - col_tap : 2 - col_tap + col_count
            ]
            total = total + jnp.einsum(
                "oc,kioj->kicj",
                weight[3 * row_tap + col_tap],
                window,
                preferred_element_type=jnp.float32,
            )
    return total


def on_device(planes, cotangent, conv_weight, context_gain, step_index):
    row_count = planes.shape[1]
    local_channels = planes.shape[2]
    col_count = planes.shape[3]
    side_cells = row_count * lax.axis_size("band")
    first_row = lax.axis_index("band") * row_count
    whole = lax.all_gather(planes, "pc", axis=2, tiled=True)
    gathered = with_halo(whole, (("band", 1),), 1)
    padded = jnp.pad(gathered, ((0, 0), (0, 0), (0, 0), (1, 1)))
    inputs = planes.astype(jnp.float32)
    gain_vec = context_gain.astype(jnp.float32)[None, None, :, None]
    channel_ids = lax.axis_index("pc") * local_channels + jnp.arange(
        local_channels, dtype=jnp.int32
    )
    time_vec = time_embed(step_index, channel_ids, C)[None, None, :, None]
    pre_act = (
        convolve(padded, conv_weight, row_count, col_count)
        + gain_vec * context(inputs, first_row, side_cells)
        + time_vec
    )
    block_out = (inputs + jax.nn.silu(pre_act)).astype(jnp.bfloat16)
    sigma_z = jax.nn.sigmoid(pre_act)
    grad_z = (cotangent.astype(jnp.float32) * sigma_z * (1.0 + pre_act * (1.0 - sigma_z))).astype(
        jnp.bfloat16
    )
    grad_rim = with_halo(grad_z, (("band", 1),), 1)
    grad_rim = jnp.pad(grad_rim, ((0, 0), (0, 0), (0, 0), (1, 1)))
    all_grads, all_weights = (
        lax.all_gather(grad_rim, "pc", axis=2, tiled=True),
        lax.all_gather(conv_weight, "pc", axis=1, tiled=True),
    )
    own_weights = lax.dynamic_slice_in_dim(
        all_weights, lax.axis_index("pc") * local_channels, local_channels, 2
    )
    conv_back = transposed(all_grads, own_weights, row_count, col_count)
    context_back = context(gain_vec * grad_z.astype(jnp.float32), first_row, side_cells)
    input_grad = (cotangent.astype(jnp.float32) + conv_back + context_back).astype(jnp.bfloat16)
    weight_terms = []
    for row_tap in range(3):
        for col_tap in range(3):
            window = padded[:, row_tap : row_tap + row_count, :, col_tap : col_tap + col_count]
            weight_terms.append(
                jnp.einsum("kioj,kicj->oc", grad_z, window, preferred_element_type=jnp.float32)
            )
    weight_grad = lax.psum_scatter(jnp.stack(weight_terms), "band", scatter_dimension=2, tiled=True)
    return (block_out, input_grad, weight_grad)


def solution(mesh):
    in_specs = (
        P(None, "band", "pc", None),
        P(None, "band", "pc", None),
        P(None, "pc", None),
        P("pc"),
        P(),
    )
    out_specs = (P(None, "band", "pc", None), P(None, "band", "pc", None), P(None, "pc", "band"))
    return jax.shard_map(
        on_device, mesh=mesh, in_specs=in_specs, out_specs=out_specs, check_vma=False
    )
```

profile of v0, /device:TPU:4, one launch (start us, length us, event | category | flops | bytes accessed | tf_op | source)
XLA Modules:
  0.0 1482.2 jit_solution(5976371227544056289)
XLA Ops:
  8.1 1.9 convert_reduce_fusion.1
  10.0 0.5 all-gather.6.cloned.1.call-update
  10.6 159.6 %all-gather = f32[1,256,64]{2,0,1:T(1,128)S(1)} all-gather(f32[1,4,64]{2,0,1:T(1,128)S(1)} %bitcast.261), channel_id=2, replica_groups=mesh['band'=64,'pc'=4] {'band'}, dimensions={1}, use_global_device_ids=true | all-gather | bytes 66560 | tf_op jit(solution)/shard_map/all_gather | solution.py:36
  170.2 0.1 copy.82
  171.0 0.7 convert_element_type.40
  171.7 385.7 %all-reduce.5.cloned.1.call-done = f32[3,64,256]{2,1,0:T(8,128)} async-done(((f32[3,64,256]{2,1,0:T(8,128)}), f32[3,64,256]{2,1,0:T(8,128)}) %all-reduce.5.cloned.1.call-update) | async-done | bytes 196624 | tf_op jit(solution)/shard_map/psum | solution.py:35
  557.4 0.9 slice_bitcast_fusion.3
  558.3 0.1 constant_dynamic-slice_fusion.1
  558.5 0.1 broadcast_add_fusion.3
  558.7 1.3 fusion.203
  560.0 1.3 collective-permute-start
  561.3 1.3 collective-permute-start.1
  562.6 0.1 broadcast_add_fusion.4
  562.7 0.4 fusion.159
  563.1 3.4 collective-permute-done
  566.6 4.5 collective-permute-done.1
  571.1 2.4 fusion.5
  573.5 0.4 fusion.161
  573.8 0.7 fusion.163
  574.5 0.7 fusion.152
  575.2 0.4 fusion.156
  575.6 2.9 fusion.202
  578.5 0.3 pad_maximum_fusion.1
  578.8 0.4 fusion.165
  579.2 0.4 fusion.154
  579.6 0.5 fusion.81
  580.1 0.5 copy-done.2
  580.6 0.1 copy-done.4
  580.7 2.6 fusion.151
  583.3 0.6 fusion.91
  583.9 0.6 fusion.97
  584.5 0.6 fusion.103
  585.1 0.6 fusion.109
  585.7 0.6 fusion.115
  586.3 0.6 fusion.121
  586.9 0.6 fusion.127
  587.5 0.6 fusion.133
  588.1 0.6 fusion.139
  588.7 2.5 copy.106
  591.3 0.5 all-gather.10.cloned.1.call-update
  591.9 2.9 collective-permute-start.2
  594.8 1.3 collective-permute-start.3
  596.1 0.9 collective-permute-done.2
  597.0 4.4 collective-permute-done.3
  601.4 1.4 fusion.146
  602.8 156.1 %all-gather.1 = f32[1,256,64]{2,0,1:T(1,128)S(1)} all-gather(f32[1,4,64]{2,0,1:T(1,128)S(1)} %bitcast.262), channel_id=3, replica_groups=mesh['band'=64,'pc'=4] {'band'}, dimensions={1}, use_global_device_ids=true | all-gather | bytes 66560 | tf_op jit(solution)/shard_map/all_gather | solution.py:36
  758.9 0.1 copy.86
  759.0 0.1 broadcast_add_fusion.2
  759.1 379.7 %all-reduce.7.cloned.1.call-done = f32[3,64,256]{2,1,0:T(8,128)} async-done(((f32[3,64,256]{2,1,0:T(8,128)}), f32[3,64,256]{2,1,0:T(8,128)}) %all-reduce.7.cloned.1.call-update) | async-done | bytes 196624 | tf_op jit(solution)/shard_map/psum | solution.py:35
  1138.8 0.9 slice_bitcast_fusion.1
  1139.8 0.1 constant_dynamic-slice_fusion
  1139.9 0.1 broadcast_add_fusion.1
  1140.0 0.1 broadcast_add_fusion
  1140.1 317.1 %reduce-scatter.2.cloned.1.call-done = f32[9,64,4]{1,0,2:T(8,128)} async-done(((f32[9,64,256]{1,0,2:T(8,128)}), f32[9,64,4]{1,0,2:T(8,128)}) %reduce-scatter.2.cloned.1.call-update) | async-done | bytes 9232 | tf_op jit(solution)/shard_map/reduce_scatter | solution.py:124
  1457.2 1.4 copy.107
  1458.6 2.6 fusion.11
  1461.2 1.9 fusion.13
  1463.1 1.6 fusion.15
  1464.7 1.6 fusion.17
  1466.3 1.3 fusion.19
  1467.7 1.6 fusion.21
  1469.3 1.6 fusion.9
  1470.9 1.3 fusion.7
  1472.2 2.6 fusion.85
  (29 shorter events, 0.6 us)
Async XLA Ops:
  8.0 163.7 %copy-start.5 = (bf16[64]{0:T(256)(128)(2,1)S(1)}, bf16[64]{0:T(256)(128)(2,1)}, u32[]{:S(2)}) copy-start(bf16[64]{0:T(256)(128)(2,1)} %param.8) | copy-start | bytes 388
  8.0 549.4 %all-reduce.5.cloned.1.call-start = ((), (), s32[]{:S(2)}) async-start(), calls=%async_computation.2 | async-start | bytes 393216 | tf_op jit(solution)/shard_map/psum | solution.py:35
  9.9 548.7 %all-gather.6.cloned.1.call-start = ((), (), s32[]{:S(2)}) async-start(), calls=%async_computation.1 | async-start | bytes 1966080 | tf_op jit(solution)/shard_map/all_gather | solution.py:86
  10.5 1128.3 %all-reduce.7.cloned.1.call-start = ((), (), s32[]{:S(2)}) async-start(), calls=%async_computation.5 | async-start | bytes 393216 | tf_op jit(solution)/shard_map/psum | solution.py:35
  170.3 392.4 %copy-start.3 = (bf16[9,64,256]{2,1,0:T(8,128)(2,1)S(1)}, bf16[9,64,256]{2,1,0:T(8,128)(2,1)}, u32[]{:S(2)}) copy-start(bf16[9,64,256]{2,1,0:T(8,128)(2,1)} %param.7) | copy-start | bytes 884740
  558.7 4.0 copy-start.1
  560.0 6.6 collective-permute-start
  561.3 9.7 collective-permute-start.1
  579.6 1.0 copy-start.2
  579.6 1.1 copy-start.4
  588.1 869.1 %reduce-scatter.2.cloned.1.call-start = ((), (), s32[]{:S(2)}) async-start(), calls=%async_computation.6 | async-start | bytes 2129920 | tf_op jit(solution)/shard_map/reduce_scatter | solution.py:124
  591.2 867.4 %all-gather.10.cloned.1.call-start = ((), (), s32[]{:S(2)}) async-start(), calls=%async_computation.4 | async-start | bytes 1474560 | tf_op jit(solution)/shard_map/all_gather | solution.py:109
  591.8 866.8 %all-gather.8.cloned.1.call-start = ((), (), s32[]{:S(2)}) async-start(), calls=%async_computation.3 | async-start | bytes 4423680 | tf_op jit(solution)/shard_map/all_gather | solution.py:108
  591.9 5.1 collective-permute-start.2
  594.8 6.6 collective-permute-start.3
  1458.6 4.5 copy-start
Sparse Core Ops, SparseCore 0:
  12.0 545.3 all-reduce.4
  588.2 550.5 all-reduce.6
  1141.3 315.8 reduce-scatter.1
Sparse Core Ops, SparseCore 1:
  12.4 26.7 all-gather.5
  593.6 25.2 all-gather.9
  620.8 37.0 all-gather.7
where the time goes:
time: 1480 us
  waiting for transfers between devices  1100 us (74%)
  blocking collectives  316 us (21%)
  matrix products  27.9 us (2%)
  between operations  16.4 us (1%)
    psum x2, waiting for transfers between devices, pooled(): totals = lax.psum(col_sums, 'band')  765 us
    reduce_scatter x1, waiting for transfers between devices, on_device(): lax.psum_scatter(jnp.stack(weight_terms), 'band', scatter_dimension=2, ti...  317 us
    all_gather x2, blocking collectives, pooled(): row_sums_all = lax.all_gather(row_sums[2], 'band', axis=0, tiled=True)  316 us
  transfers between devices with their start and end apart: 10, of which 7 were waited for; matrix products, arithmetic and copies ran while one was open for 1% of the time, Pallas kernels for 0%

commit v1 on v0

--- a/solution.py
+++ b/solution.py
@@ -32,7 +32,7 @@
 def pooled(values):
     col_sums = jnp.sum(values, axis=1)
     row_sums = jnp.sum(values, axis=3)
-    totals = lax.psum(col_sums, "band")
+    totals = jax.lax.all_gather(col_sums, "band").sum(axis=0)
     row_sums_all = lax.all_gather(row_sums[2], "band", axis=0, tiled=True)
     return (totals, row_sums, row_sums_all)
 

time: 1480 us -> 1120 us (0.76)
  waiting for transfers between devices: 1100 us -> 685 us
  other arithmetic: 7.15 us -> 25.5 us
  matrix products: 27.9 us -> 43.5 us
    psum x2 -> x0, waiting for transfers between devices: 765 us -> none  [pooled(): totals = lax.psum(col_sums, 'band')]
    all_gather x0 -> x2, waiting for transfers between devices: none -> 448 us  [pooled(): totals = jax.lax.all_gather(col_sums, 'band').sum(axis=0)]
    reduce_scatter x1, waiting for transfers between devices: 317 us -> 147 us  [on_device(): lax.psum_scatter(jnp.stack(weight_terms), 'band', scatter_dimension=2, ti...]
    all_gather x1, waiting for transfers between devices: 0.01 us -> 38.7 us  [on_device(): lax.all_gather(grad_rim, 'pc', axis=2, tiled=True)]
    all_gather x1, waiting for transfers between devices: 0.03 us -> 25.8 us  [on_device(): whole = lax.all_gather(planes, 'pc', axis=2, tiled=True)]
    all_gather x1, waiting for transfers between devices: 0.01 us -> 18.7 us  [on_device(): lax.all_gather(conv_weight, 'pc', axis=1, tiled=True)]
  transfers between devices with their start and end apart: 10 -> 10, of which waited for: 7 -> 8; matrix products, arithmetic and copies ran while one was open for 1% -> 4% of each run, Pallas kernels for 0% -> 0%
where the time goes in v1:
time: 1120 us
  waiting for transfers between devices  685 us (61%)
  blocking collectives  313 us (28%)
  matrix products  43.5 us (4%)
  other arithmetic  25.5 us (2%)
  local copies, waits for them, and re-layouts  24 us (2%)
  between operations  15.1 us (1%)
    all_gather x2, waiting for transfers between devices, pooled(): totals = jax.lax.all_gather(col_sums, 'band').sum(axis=0)  448 us
    all_gather x2, blocking collectives, pooled(): row_sums_all = lax.all_gather(row_sums[2], 'band', axis=0, tiled=True)  313 us
    reduce_scatter x1, waiting for transfers between devices, on_device(): lax.psum_scatter(jnp.stack(weight_terms), 'band', scatter_dimension=2, ti...  147 us
    all_gather x1, waiting for transfers between devices, on_device(): lax.all_gather(grad_rim, 'pc', axis=2, tiled=True)  38.7 us
    all_gather x1, waiting for transfers between devices, on_device(): whole = lax.all_gather(planes, 'pc', axis=2, tiled=True)  25.8 us
    dot_general x9, matrix products, transposed(): jnp.einsum('oc,kioj->kicj', weight[3 * row_tap + col_tap], window, prefer...  25.3 us
  transfers between devices with their start and end apart: 10, of which 8 were waited for; matrix products, arithmetic and copies ran while one was open for 4% of the time, Pallas kernels for 0%

profile of v1, /device:TPU:4, one launch (start us, length us, event | category | flops | bytes accessed | tf_op | source)
XLA Modules:
  0.0 1115.7 jit_solution(14229017320800293305)
XLA Ops:
  7.2 0.7 all-gather.10.cloned.1.call-update
  8.0 1.9 convert_reduce_fusion.1
  10.6 25.8 %all-gather.10.cloned.1.call-done = bf16[3,4,256,256]{3,2,1,0:T(8,128)(2,1)} async-done(((bf16[3,4,64,256]{3,2,1,0:T(8,128)(2,1)}), bf16[3,4,256,256]{3,2,1,0:T(8,128)(2,1)}) %all-gather.10.cloned.1.call-update) | async-done | bytes 1572880 | tf_op jit(solution)/shard_map/all_gather | solution.py:86
  36.4 1.3 fusion.203
  37.7 3.7 collective-permute-start
  41.3 1.3 collective-permute-start.1
  42.6 0.7 compare_select_fusion
  43.8 158.7 %all-gather = f32[1,256,64]{2,0,1:T(1,128)S(1)} all-gather(f32[1,4,64]{2,0,1:T(1,128)S(1)} %bitcast.265), channel_id=2, replica_groups=mesh['band'=64,'pc'=4] {'band'}, dimensions={1}, use_global_device_ids=true | all-gather | bytes 66560 | tf_op jit(solution)/shard_map/all_gather | solution.py:36
  202.5 0.7 copy.84
  203.2 1.1 fusion.159
  204.4 0.7 copy-done.14
  205.1 0.7 copy-done.15
  206.2 4.0 fusion.5
  210.6 0.7 fusion.163
  211.3 1.6 fusion.152
  212.8 1.3 fusion.156
  214.5 1.3 fusion.154
  215.8 1.4 fusion.81
  217.2 5.1 fusion.202
  222.3 141.5 %all-gather.16.cloned.1.call-done = f32[192,64,256]{2,1,0:T(8,128)} async-done(((f32[3,64,256]{2,1,0:T(8,128)}), f32[192,64,256]{2,1,0:T(8,128)}) %all-gather.16.cloned.1.call-update) | async-done | bytes 12582928 | tf_op jit(solution)/shard_map/all_gather | solution.py:35
  363.8 6.1 reduce_sum.56
  369.9 1.6 slice_bitcast_fusion.3
  371.4 0.7 constant_dynamic-slice_fusion.1
  372.1 0.8 copy.85
  373.0 0.9 broadcast_add_fusion.4
  373.9 1.0 broadcast_add_fusion.3
  374.9 4.8 fusion.151
  380.3 1.0 copy-done.7
  381.9 0.8 copy-done.12
  384.0 0.7 copy-done.3
  384.7 0.6 fusion.115
  385.3 0.8 copy-done.10
  386.1 0.6 fusion.121
  387.4 0.7 copy-done.5
  388.1 0.6 fusion.133
  388.7 0.8 copy-done.8
  390.1 2.5 copy.108
  393.6 2.5 collective-permute-start.2
  396.1 1.3 collective-permute-start.3
  397.4 0.9 collective-permute-done.2
  398.3 4.3 collective-permute-done.3
  402.7 1.4 fusion.146
  404.6 154.5 %all-gather.2 = f32[1,256,64]{2,0,1:T(1,128)S(1)} all-gather(f32[1,4,64]{2,0,1:T(1,128)S(1)} %bitcast.266), channel_id=4, replica_groups=mesh['band'=64,'pc'=4] {'band'}, dimensions={1}, use_global_device_ids=true | all-gather | bytes 66560 | tf_op jit(solution)/shard_map/all_gather | solution.py:36
  559.3 0.8 broadcast_add_fusion.2
  560.1 147.5 %reduce-scatter.2.cloned.1.call-done = f32[9,64,4]{1,0,2:T(8,128)} async-done(((f32[9,64,256]{1,0,2:T(8,128)}), f32[9,64,4]{1,0,2:T(8,128)}) %reduce-scatter.2.cloned.1.call-update) | async-done | bytes 9232 | tf_op jit(solution)/shard_map/reduce_scatter | solution.py:124
  707.5 1.4 copy.109
  708.9 18.7 %all-gather.14.cloned.1.call-done = bf16[9,256,256]{2,1,0:T(8,128)(2,1)} async-done(((bf16[9,64,256]{2,1,0:T(8,128)(2,1)}), bf16[9,256,256]{2,1,0:T(8,128)(2,1)}) %all-gather.14.cloned.1.call-update) | async-done | bytes 1179664 | tf_op jit(solution)/shard_map/all_gather | solution.py:109
  727.6 38.7 %all-gather.12.cloned.1.call-done = bf16[3,6,256,258]{3,2,1,0:T(8,128)(2,1)} async-done(((bf16[3,6,64,258]{3,2,1,0:T(8,128)(2,1)}), bf16[3,6,256,258]{3,2,1,0:T(8,128)(2,1)}) %all-gather.12.cloned.1.call-update) | async-done | bytes 2377744 | tf_op jit(solution)/shard_map/all_gather | solution.py:108
  766.2 3.5 fusion.11
  769.7 2.8 fusion.13
  772.5 2.5 fusion.15
  775.0 2.5 fusion.17
  777.5 2.2 fusion.19
  779.7 2.5 fusion.21
  782.1 2.5 fusion.9
  784.6 2.2 fusion.7
  786.9 306.2 %all-gather.18.cloned.1.call-done = f32[192,64,256]{2,1,0:T(8,128)} async-done(((f32[3,64,256]{2,1,0:T(8,128)}), f32[192,64,256]{2,1,0:T(8,128)}) %all-gather.18.cloned.1.call-update) | async-done | bytes 12582928 | tf_op jit(solution)/shard_map/all_gather | solution.py:35
  1093.1 6.1 reduce_sum.59
  1099.2 1.6 slice_bitcast_fusion.1
  1100.7 0.7 constant_dynamic-slice_fusion
  1101.4 0.8 copy.89
  1102.3 0.9 broadcast_add_fusion.1
  1103.2 0.9 broadcast_add_fusion
  1104.2 4.7 fusion.85
  (59 shorter events, 7.2 us)
Async XLA Ops:
  7.2 35.5 %copy-start.19 = (bf16[64]{0:T(256)(128)(2,1)S(1)}, bf16[64]{0:T(256)(128)(2,1)}, u32[]{:S(2)}) copy-start(bf16[64]{0:T(256)(128)(2,1)} %param.8) | copy-start | bytes 388
  7.2 29.2 %all-gather.10.cloned.1.call-start = ((), (), s32[]{:S(2)}) async-start(), calls=%async_computation.1 | async-start | bytes 1966080 | tf_op jit(solution)/shard_map/all_gather | solution.py:86
  7.9 355.9 %all-gather.16.cloned.1.call-start = ((), (), s32[]{:S(2)}) async-start(), calls=%async_computation.5 | async-start | bytes 12779520 | tf_op jit(solution)/shard_map/all_gather | solution.py:35
  9.8 697.7 %reduce-scatter.2.cloned.1.call-start = ((), (), s32[]{:S(2)}) async-start(), calls=%async_computation.4 | async-start | bytes 2129920 | tf_op jit(solution)/shard_map/reduce_scatter | solution.py:124
  36.4 166.8 %copy-start.1 = (bf16[3,4,256,256]{3,2,1,0:T(8,128)(2,1)S(1)}, bf16[3,4,256,256]{3,2,1,0:T(8,128)(2,1)}, u32[]{:S(2)}) copy-start(bf16[3,4,256,256]{3,2,1,0:T(8,128)(2,1)} %all-gather.10.cloned.1.call-done) | copy-start | bytes 4718596
  37.7 166.7 %collective-permute-start = (bf16[3,1,256,256]{3,2,1,0:T(8,128)(2,1)S(1)}, bf16[3,1,256,256]{3,2,1,0:T(8,128)(2,1)S(1)}, u32[]{:S(2)}, u32[]{:S(2)}) collective-permute-start(bf16[3,1,256,256]{3,2,1,0:T(8,128)(2,1)S(1)} %get-tuple-element.28), channel_id=1, source_target_pairs={{0,4},{4,8},{8,12},{12,16},{16,20},{20,24},{24,28},{28,32},{32,36}... | collective-permute-start | bytes 1179656 | tf_op jit(solution)/shard_map/ppermute | solution.py:15
  41.3 163.0 %collective-permute-start.1 = (bf16[3,1,256,256]{3,2,1,0:T(8,128)(2,1)S(1)}, bf16[3,1,256,256]{3,2,1,0:T(8,128)(2,1)S(1)}, u32[]{:S(2)}, u32[]{:S(2)}) collective-permute-start(bf16[3,1,256,256]{3,2,1,0:T(8,128)(2,1)S(1)} %get-tuple-element.29), channel_id=1, source_target_pairs={{4,0},{8,4},{12,8},{16,12},{20,16},{24,20},{28,24},{32,28},{36,32}... | collective-permute-start | bytes 1179656 | tf_op jit(solution)/shard_map/ppermute | solution.py:18
  204.3 1.8 copy-start.2
  204.3 0.7 copy-start.14
  205.1 0.7 copy-start.15
  206.1 8.0 copy-start.6
  206.1 8.4 copy-start.4
  206.1 4.0 copy-start.16
  374.9 4.8 copy-start.13
  379.7 9.0 copy-start.17
  379.7 1.5 copy-start.7
  381.3 1.4 copy-start.12
  381.9 1.5 copy-start.11
  383.3 1.4 copy-start.3
  384.7 1.4 copy-start.10
  385.3 1.5 copy-start.9
  386.7 1.4 copy-start.5
  388.1 1.4 copy-start.8
  392.6 1.0 copy-start.18
  392.6 334.9 %all-gather.14.cloned.1.call-start = ((), (), s32[]{:S(2)}) async-start(), calls=%async_computation.3 | async-start | bytes 1474560 | tf_op jit(solution)/shard_map/all_gather | solution.py:109
  393.2 373.0 %all-gather.12.cloned.1.call-start = ((), (), s32[]{:S(2)}) async-start(), calls=%async_computation.2 | async-start | bytes 4423680 | tf_op jit(solution)/shard_map/all_gather | solution.py:108
  393.6 4.7 collective-permute-start.2
  396.1 6.5 collective-permute-start.3
  404.1 689.0 %all-gather.18.cloned.1.call-start = ((), (), s32[]{:S(2)}) async-start(), calls=%async_computation.6 | async-start | bytes 12779520 | tf_op jit(solution)/shard_map/all_gather | solution.py:35
  766.2 6.3 copy-start
Sparse Core Ops, SparseCore 0:
  9.8 26.4 all-gather.9
  38.1 325.5 all-gather.15
  392.8 314.7 reduce-scatter.1
  709.3 18.1 all-gather.13
  729.4 36.8 all-gather.11
  768.0 325.0 all-gather.17
